TPU v7x, 32 devices: a whole 2x2x4 slice. The times are simulated.
32 devices in a mesh: parts: 2 (over x), scan: 16 (over z, y, core).
Axes of the slice: x: 2, y: 2, z: 4, core: 2. Of those that a mesh axis runs over, the one named last changes fastest.
Arguments:
- object_slices: float32 [4, 2, 4096, 256], P('parts', None, 'scan'), parts along dimension 0, may hold values from -4 to 4
- probe_modes: float32 [8, 2, 128, 128], P('parts'), parts along dimension 0, may hold values from -4 to 4
- propagator_phase: float32 [128, 128], replicated, may hold values from -3.140625 to 3.140625
- measured: float32 [256, 128, 128], P(('parts', 'scan')), parts along dimension 0, may hold values from 0.5 to 3
- positions: int32 [256, 2], P(('parts', 'scan')), parts along dimension 0, may hold values from 0 to 3839, as said below
- live_count: int32 [32], P(('parts', 'scan')), parts along dimension 0, may hold values from 1 to 8, as said below
Outputs:
- object_gradient: float32 [4, 2, 4096, 256], P('parts', None, 'scan'), parts along dimension 0
- probe_gradient: float32 [8, 2, 128, 128], P('parts'), parts along dimension 0
- position_loss: float32 [256], P(('parts', 'scan')), parts along dimension 0
There are 2 independent parts, one for each index of `parts`. A program takes and returns all parts, laid end to end along the dimension named above; an argument that names none is the same for every part. Nothing has to cross between parts.
Inputs may be any that keep to these rules, and one draw needn't show every extreme that they name: `positions`: object tile k is rows k * 256 to (k + 1) * 256 - 1. Slots s * 8 to (s + 1) * 8 - 1 belong to scan owner s; each of their windows lies within tiles s - 2 to s + 2 and never in the last tile alone; columns start at 0 to 128. Every owner has a slot in tile max(s - 2, 0) and a slot whose window reaches tile min(s + 2, 16 - 1). `live_count`: live slots of an owner come first; some owner is full in every draw.
All inputs are finite; a program needn't handle non-finite values.
Results may differ from a plain program's by a relative error of at most 0.0003.
Values sent between devices are 32-bit elements; how exact they have to be, the bound alone decides.
No kernel may reach another device: no remote copies, remote signals or barrier semaphores. Data moves between devices by JAX's collectives and lax.ppermute only.
A program may use at most 128 MiB of HBM per device.

v0:
```python
import functools
import math

import jax
import jax.numpy as jnp
import numpy as np
from jax import lax
from jax.experimental import pallas as pl
from jax.experimental.pallas import tpu as pltpu
from jax.sharding import PartitionSpec as P

F32 = jnp.float32
BF16 = jnp.bfloat16
LOSS_PAD = 16
VMEM_LIMIT = 48 * 1024 * 1024
HBM = pl.BlockSpec(memory_space=pl.ANY)
VMEM = pl.BlockSpec(memory_space=pltpu.VMEM)
SMEM = pl.BlockSpec(memory_space=pltpu.SMEM)


def shifted(value, axis, steps):
    count = lax.axis_size(axis)
    first, last = (max(0, -steps), min(count, count - steps))
    return lax.ppermute(value, axis, [(source, source + steps) for source in range(first, last)])


def swapped(value, axis, bit):
    count = lax.axis_size(axis)
    return lax.ppermute(value, axis, [(source, source ^ bit) for source in range(count)])


def fourier_table(size):
    counter = np.arange(size)
    angles = (counter[:, None] * counter[None, :] % size) * (2.0 * math.pi / size)
    return np.stack([np.cos(angles), np.sin(angles)]).astype(np.float32) / np.float32(math.sqrt(size))


class Mover:
    def __init__(self, sem):
        self.sem, self.copies, self.used = sem, [], 0

    def __call__(self, source, target):
        copy = pltpu.make_async_copy(source, target, self.sem.at[self.used])
        copy.start()
        self.copies.append(copy)
        self.used += 1

    def wait(self):
        for copy in self.copies:
            copy.wait()
        self.copies = []


def facts_kernel(slots, corners, live, measured, out):
    rows, size = measured.shape
    out[:rows] = measured[...]
    lane = lax.broadcasted_iota(jnp.int32, (8, size), 1)
    line = lax.broadcasted_iota(jnp.int32, (8, size), 0)
    value = jnp.zeros((8, size), jnp.int32)
    for s in range(slots):
        alive = (live[0] > s).astype(jnp.int32)
        fact = jnp.where(lane == 0, corners[0, s], jnp.where(lane == 1, corners[1, s], alive))
        value = jnp.where(jnp.logical_and(line == s, lane < 3), fact, value)
    out[rows:] = value.astype(F32)


def add_halo_kernel(place, packed, own, pair, out, sem):
    rows, size = packed.shape
    half = size // 2
    core = place[0]
    for source, side in ((own, 0), (pair, 1)):

        @pl.when(core == side)
        def _():
            move = Mover(sem)
            for k in range(2):
                for ri in range(2):
                    for lanes in range(2):
                        block = pl.ds(rows + ((k * 2 + ri) * 2 + lanes) * half, half)
                        move(source.at[k, ri, pl.ds(side * half, half), pl.ds(lanes * size, size)], out.at[block])
            out[:rows] = packed[...]
            move.wait()


def with_facts(positions, live, pattern):
    rows, size = pattern.shape
    return pl.pallas_call(
        functools.partial(facts_kernel, positions.shape[0]),
        out_shape=jax.ShapeDtypeStruct((rows + 8, size), F32),
        in_specs=[SMEM, SMEM, VMEM],
        out_specs=VMEM,
    )(positions.T, live, pattern)


def add_halo(place, packed, own, pair):
    rows, size = packed.shape
    return pl.pallas_call(
        add_halo_kernel,
        out_shape=jax.ShapeDtypeStruct((rows + 4 * size, size), F32),
        in_specs=[SMEM, VMEM, HBM, VMEM],
        out_specs=VMEM,
        scratch_shapes=[pltpu.SemaphoreType.DMA((8,))],
    )(place, packed, own, pair)


def kernel(
    early, size, modes, slots, tile, place, own, pair, packs, before, wave_ref, prop_ref, table_ref, outs, sums_ref,
    obj, acc, pat, written, whole, facts, todo, tables, cells, cgrad, wave1, far, ops, sem,
):
    core = place[0]
    chip_top = place[1]
    first_id = place[2]
    half = size // 2
    rows = slots * size
    top = pl.multiple_of(core * tile, tile)
    other = pl.multiple_of(tile - core * tile, tile)
    limit = 2 * tile - size
    first_group = 1 if early else 0

    move = Mover(sem)
    for i, source in enumerate(packs):
        move(source.at[pl.ds(rows, 8)], written.at[i])
    facts_in = move.copies
    move.copies = []
    move(own, obj.at[:, :, pl.ds(top, tile)])
    move(pair, obj.at[:, :, pl.ds(other, tile)])
    for i, source in enumerate(packs):
        move(source.at[pl.ds(0, rows)], pat.at[i])
    if early:
        acc[...] = jnp.zeros_like(acc)
        sums_ref[...] = jnp.zeros_like(sums_ref)
    else:
        for k in range(2):
            for ri in range(2):
                for side in range(2):
                    block = pl.ds(rows + 8 + ((k * 2 + ri) * 2 + side) * half, half)
                    lanes = pl.ds(side * size, size)
                    near = pl.multiple_of(2 * tile + core * half, half)
                    far_off = pl.multiple_of(2 * tile + half - core * half, half)
                    move(packs[4].at[block], obj.at[k, ri, pl.ds(near, half), lanes])
                    move(packs[5].at[block], obj.at[k, ri, pl.ds(far_off, half), lanes])
        old_grad, old_sums = before
        move(old_grad, acc.at[:, :, pl.ds(0, 2 * tile)])
        move(old_sums, sums_ref)
        acc[:, :, 2 * tile:] = jnp.zeros((2, 2, size, acc.shape[3]), F32)

    right_f, right_g, left_f, left_g = (tables.at[i] for i in range(4))
    cosine, sine = table_ref[0], table_ref[1]
    for index, part in enumerate(("high", "high", "low")):
        def cut(value):
            high = value.astype(BF16)
            return high if part == "high" else (value - high.astype(F32)).astype(BF16)
        c, s, n = cut(cosine), cut(sine), cut(-sine)
        base = index * 2 * size
        one, two = pl.ds(0, size), pl.ds(size, size)
        for kind, (a, b, d, e) in ((0, (c, n, s, c)), (1, (c, s, n, c))):
            tables[kind, pl.ds(base, size), one] = a
            tables[kind, pl.ds(base, size), two] = b
            tables[kind, pl.ds(base + size, size), one] = d
            tables[kind, pl.ds(base + size, size), two] = e

    def square(kind, part):
        return tables[kind, pl.ds(part * 2 * size, 2 * size), :]

    mat = functools.partial(jnp.dot, preferred_element_type=F32)
    (r1, l1, l2, r2, r3, l3, l4, r4, r5, l5, l6, r6) = range(12)
    pairs = range(modes // 2)

    def split(b, stage, at, value):
        high = value.astype(BF16)
        ops.at[b, stage, 0][at] = high
        ops.at[b, stage, 1][at] = (value - high.astype(F32)).astype(BF16)

    def put_right(b, stage, m, real, imag):
        split(b, stage, (pl.ds(m * size, size), pl.ds(0, size)), real)
        split(b, stage, (pl.ds(m * size, size), pl.ds(size, size)), imag)

    def right(b, stage, m, kind):
        at = (pl.ds(m * size, size), pl.ds(0, 2 * size))
        high, low = ops.at[b, stage, 0][at], ops.at[b, stage, 1][at]
        out = mat(jnp.concatenate([high, low, high], 1), tables[kind])
        return out[:, :size], out[:, size:]

    def put_left(b, stage, m, real, imag):
        base = (m // 2) * 2 * size
        lanes = pl.ds((m % 2) * size, size)
        split(b, stage, (pl.ds(base, size), lanes), real)
        split(b, stage, (pl.ds(base + size, size), lanes), imag)

    def left(b, stage, p, kind):
        at = (pl.ds(p * 2 * size, 2 * size), pl.ds(0, 2 * size))
        high, low = ops.at[b, stage, 0][at], ops.at[b, stage, 1][at]
        wide = jnp.concatenate([square(1 - kind, 0), square(1 - kind, 0), square(1 - kind, 2)], 1)
        out = mat(wide, jnp.concatenate([high, low, high], 0))
        return [(out[:size, j * size:(j + 1) * size], out[size:, j * size:(j + 1) * size]) for j in range(2)]

    def where_of(slot):
        group, owner, place_in = slot // (2 * slots), (slot // slots) % 2, slot % slots
        return 2 * (group - first_group) + (owner + core - 2 * owner * core), place_in

    def window(b, job):
        slot = todo[3 * job]
        row = todo[3 * job + 1]
        column = todo[3 * job + 2]
        base = pl.multiple_of(lax.div(row, 8) * 8, 8)
        ahead = row - base
        tall = size + 8
        for k in range(2):
            for ri in range(2):
                value = obj[k, ri, pl.ds(base, tall), :]
                value = pltpu.roll(value, 2 * size - column, 1)[:, :size]
                cells[b, k, ri] = pltpu.roll(value, tall - ahead, 0)[:size]
        yield
        for m in range(modes):
            pr, pi = wave_ref[m, 0], wave_ref[m, 1]
            o_r, o_i = cells[b, 0, 0], cells[b, 0, 1]
            put_right(b, r1, m, pr * o_r - pi * o_i, pr * o_i + pi * o_r)
        yield
        for m in range(modes):
            put_left(b, l1, m, *right(b, r1, m, 0))
        yield
        for p in pairs:
            for j, (re, im) in enumerate(left(b, l1, p, 0)):
                h_r, h_i = prop_ref[0], prop_ref[1]
                put_left(b, l2, 2 * p + j, re * h_r - im * h_i, re * h_i + im * h_r)
        yield
        for p in pairs:
            for j, (re, im) in enumerate(left(b, l2, p, 1)):
                put_right(b, r2, 2 * p + j, re, im)
        yield
        for m in range(modes):
            re, im = right(b, r2, m, 1)
            wave1[b, m, 0] = re
            wave1[b, m, 1] = im
            o_r, o_i = cells[b, 1, 0], cells[b, 1, 1]
            put_right(b, r3, m, re * o_r - im * o_i, re * o_i + im * o_r)
        yield
        for m in range(modes):
            put_left(b, l3, m, *right(b, r3, m, 0))
        yield
        for p in pairs:
            for j, (re, im) in enumerate(left(b, l3, p, 0)):
                far[b, 2 * p + j, 0] = re
                far[b, 2 * p + j, 1] = im
        yield
        total = jnp.zeros((size, size), F32)
        for m in range(modes):
            re, im = far[b, m, 0], far[b, m, 1]
            total = total + (re * re + im * im)
        buffer, line = where_of(slot)
        target = pat[buffer, pl.ds(pl.multiple_of(line * size, size), size), :]
        amplitude = jnp.sqrt(total + 0.5)
        residual = amplitude - target
        loss = 0.5 * jnp.sum(residual * residual) * (2.0 / (size * size))
        ratio = residual / amplitude
        spot = lax.broadcasted_iota(jnp.int32, (8, size), 0) * size + lax.broadcasted_iota(jnp.int32, (8, size), 1)
        for end in (1, 2):
            at = (pl.ds(end * modes * size + (end - 1) * LOSS_PAD, 8), pl.ds(0, size))
            sums_ref[at] = jnp.where(spot == first_id + slot, loss, sums_ref[at])
        for m in range(modes):
            put_left(b, l4, m, far[b, m, 0] * ratio, far[b, m, 1] * ratio)
        yield
        for p in pairs:
            for j, (re, im) in enumerate(left(b, l4, p, 1)):
                put_right(b, r4, 2 * p + j, re, im)
        yield
        for m in range(modes):
            re, im = right(b, r4, m, 1)
            w_r, w_i = wave1[b, m, 0], wave1[b, m, 1]
            add_r, add_i = re * w_r + im * w_i, im * w_r - re * w_i
            if m == 0:
                cgrad[b, 1, 0] = add_r
                cgrad[b, 1, 1] = add_i
            else:
                cgrad[b, 1, 0] += add_r
                cgrad[b, 1, 1] += add_i
            o_r, o_i = cells[b, 1, 0], cells[b, 1, 1]
            put_right(b, r5, m, re * o_r + im * o_i, im * o_r - re * o_i)
        yield
        for m in range(modes):
            put_left(b, l5, m, *right(b, r5, m, 0))
        yield
        for p in pairs:
            for j, (re, im) in enumerate(left(b, l5, p, 0)):
                h_r, h_i = prop_ref[0], prop_ref[1]
                put_left(b, l6, 2 * p + j, re * h_r + im * h_i, im * h_r - re * h_i)
        yield
        for p in pairs:
            for j, (re, im) in enumerate(left(b, l6, p, 1)):
                put_right(b, r6, 2 * p + j, re, im)
        yield
        for m in range(modes):
            re, im = right(b, r6, m, 1)
            o_r, o_i = cells[b, 0, 0], cells[b, 0, 1]
            line = 2 * m * size + (2 * m // modes) * LOSS_PAD
            sums_ref[pl.ds(line, size), :] += re * o_r + im * o_i
            sums_ref[pl.ds(line + size, size), :] += im * o_r - re * o_i
            pr, pi = wave_ref[m, 0], wave_ref[m, 1]
            add_r, add_i = re * pr + im * pi, im * pr - re * pi
            if m == 0:
                cgrad[b, 0, 0] = add_r
                cgrad[b, 0, 1] = add_i
            else:
                cgrad[b, 0, 0] += add_r
                cgrad[b, 0, 1] += add_i
        yield
        for k in range(2):
            for ri in range(2):
                value = jnp.concatenate([cgrad[b, k, ri], jnp.zeros((8, size), F32)], 0)
                value = pltpu.roll(value, ahead, 0)
                value = jnp.concatenate([value, jnp.zeros_like(value)], 1)
                acc[k, ri, pl.ds(base, tall), :] += pltpu.roll(value, column, 1)

    def together(jobs):
        streams = [window(*job) for job in jobs]
        while streams:
            for stream in list(streams):
                try:
                    next(stream)
                except StopIteration:
                    streams.remove(stream)

    for copy in facts_in:
        copy.wait()
    whole[...] = written[...].astype(jnp.int32)
    move(whole, facts)
    move.copies.pop().wait()
    count = jnp.int32(0)
    number = jnp.int32(0)
    wanted = []
    for slot in range(2 * slots if early else 0, 4 * slots if early else 6 * slots):
        buffer, line = where_of(slot)
        row = facts[buffer, line, 0] - chip_top
        alive = jnp.logical_and(facts[buffer, line, 2] > 0, row >= 0)
        first = jnp.logical_and(alive, row <= limit).astype(jnp.int32)
        here = first if early else jnp.logical_and(alive, row < 2 * tile).astype(jnp.int32)
        if not early and 2 * slots <= slot < 4 * slots:
            here = here - first
            count = count + first
        wanted.append((slot, row, facts[buffer, line, 1], here))
    for slot, row, column, here in wanted:
        todo[3 * number] = jnp.int32(slot)
        todo[3 * number + 1] = row
        todo[3 * number + 2] = column
        number = number + here * (1 - lax.bitwise_xor(lax.bitwise_and(count, 1), core))
        count = count + here
    move.wait()

    def two(step, carry):
        together([(b, 2 * step + b) for b in range(2)])
        return carry

    lax.fori_loop(0, lax.div(number, 2), two, 0)

    @pl.when(lax.bitwise_and(number, 1) == 1)
    def _():
        together([(0, number - 1)])

    if early:
        move(acc.at[:, :, pl.ds(0, 2 * tile)], outs[0])
    else:
        mine_ref, theirs_ref = outs
        move(acc.at[:, :, pl.ds(top, tile)], mine_ref)
        move(acc.at[:, :, pl.ds(other, tile)], theirs_ref.at[:, :, pl.ds(0, tile)])
        move(acc.at[:, :, pl.ds(2 * tile, size)], theirs_ref.at[:, :, pl.ds(tile, size)])
    move.wait()


def flat_kernel(early, size, modes, slots, tile, counts, *refs):
    groups = []
    for count in counts:
        groups.append(refs[:count])
        refs = refs[count:]
    fixed, packs, before, inputs, outs, sums, scratch = groups
    kernel(early, size, modes, slots, tile, *fixed, packs, before, *inputs, outs, *sums, *scratch)


def windows(place, own, pair, packs, before, waves, prop, table, slots):
    modes, _, size, _ = waves.shape
    tile, columns = own.shape[2:]
    early = not before
    sums = jax.ShapeDtypeStruct((2 * modes * size + 2 * LOSS_PAD, size), F32)
    if early:
        outs = (jax.ShapeDtypeStruct((2, 2, 2 * tile, columns), F32),)
    else:
        outs = (
            jax.ShapeDtypeStruct((2, 2, tile, columns), F32),
            jax.ShapeDtypeStruct((2, 2, tile + size, columns), F32),
        )
    scratch = [
        pltpu.VMEM((2, 2, 2 * tile + size, columns), F32),
        pltpu.VMEM((2, 2, 2 * tile + size, columns), F32),
        pltpu.VMEM((len(packs), slots * size, size), F32),
        pltpu.VMEM((len(packs), 8, size), F32),
        pltpu.VMEM((len(packs), 8, size), jnp.int32),
        pltpu.SMEM((len(packs), 8, size), jnp.int32),
        pltpu.SMEM((9 * slots + 8,), jnp.int32),
        pltpu.VMEM((2, 6 * size, 2 * size), BF16),
        pltpu.VMEM((2, 2, 2, size, size), F32),
        pltpu.VMEM((2, 2, 2, size, size), F32),
        pltpu.VMEM((2, modes, 2, size, size), F32),
        pltpu.VMEM((2, modes, 2, size, size), F32),
        pltpu.VMEM((2, 12, 2, modes * size, 2 * size), BF16),
        pltpu.SemaphoreType.DMA((48,)),
    ]
    counts = (3, len(packs), len(before), 3, len(outs), 1, len(scratch))
    return pl.pallas_call(
        functools.partial(flat_kernel, early, size, modes, slots, tile, counts),
        out_shape=outs + (sums,),
        in_specs=[SMEM] + [HBM] * (2 + len(packs) + len(before)) + [VMEM] * 3,
        out_specs=(HBM,) * len(outs) + (VMEM,),
        scratch_shapes=scratch,
        compiler_params=pltpu.CompilerParams(vmem_limit_bytes=VMEM_LIMIT),
        cost_estimate=pl.CostEstimate(flops=6 * modes * 6 * 16 * size**3, bytes_accessed=8 << 20, transcendentals=0),
    )(place, own, pair, *packs, *before, waves, prop, table)


def swapped_beside(value, axis, bit, work):
    return lax.optimization_barrier((swapped(value, axis, bit), work))


def halves(value, axis, bit):
    half = value.shape[0] // 2
    side = (lax.axis_index(axis) // bit) % 2
    kept = lax.dynamic_slice_in_dim(value, side * half, half, 0)
    given = lax.dynamic_slice_in_dim(value, (1 - side) * half, half, 0)
    return kept, given


def in_order(value, got, axis, bit):
    side = (lax.axis_index(axis) // bit) % 2
    return jnp.where(side == 0, value, got), jnp.where(side == 0, got, value)


def shards(object_slices, probe_modes, propagator_phase, measured, positions, live_count):
    modes, _, size, _ = probe_modes.shape
    tile = object_slices.shape[2]
    slots = positions.shape[0]
    count = lax.axis_size("scan")
    index = lax.axis_index("scan")
    core = index % 2
    chip = index // 2
    place = jnp.stack([core, chip * 2 * tile, (chip - 1) * 2 * slots]).astype(jnp.int32)
    prop = jnp.stack([jnp.cos(propagator_phase), jnp.sin(propagator_phase)])
    table = jnp.asarray(fourier_table(size))
    pattern = measured.reshape(slots * size, size)
    pair = swapped(object_slices, "scan", 1)
    packed = with_facts(positions, live_count, pattern)
    up = shifted(packed, "scan", 2)
    pair_packed = swapped(packed, "scan", 1)
    down = shifted(add_halo(place, packed, object_slices, pair), "scan", -2)
    shared = (probe_modes, prop, table, slots)
    before = windows(place, object_slices, pair, (packed, pair_packed), (), *shared)
    before, up, down = lax.optimization_barrier((before, up, down))
    packs = (up, swapped(up, "scan", 1), packed, pair_packed, down, swapped(down, "scan", 1))
    mine, theirs, sums = windows(place, object_slices, pair, packs, before, *shared)

    kept, given = halves(sums, "scan", 1)
    sums = kept + swapped(given, "scan", 1)
    back = swapped(theirs, "scan", 1)
    halo = theirs[:, :, tile:] + back[:, :, tile:]
    kept, given = halves(sums, "scan", 2)
    got, halo = swapped_beside(given, "scan", 2, halo)
    sums = kept + got
    halo = lax.ppermute(halo, "scan", [(s, s + 1) for s in range(1, count - 1, 2)])
    grad = mine + back[:, :, :tile] + jnp.pad(halo, ((0, 0), (0, 0), (0, tile - size), (0, 0)))
    bit = 4
    while bit < count:
        if 2 * bit < count:
            got = swapped(sums, "scan", bit)
        else:
            got, grad = swapped_beside(sums, "scan", bit, grad)
        sums = sums + got
        bit *= 2
    sums = jnp.concatenate(in_order(sums, swapped(sums, "scan", 2), "scan", 2), 0)
    half = modes * size
    losses = sums[half:half + 8].reshape(-1)
    position_loss = lax.dynamic_slice_in_dim(losses, index * slots, slots, 0)
    sums = sums[:half]
    got, position_loss = swapped_beside(sums, "scan", 1, position_loss)
    probe_gradient = jnp.concatenate(in_order(sums, got, "scan", 1), 0).reshape(probe_modes.shape)
    return (grad, probe_gradient, position_loss)


def solution(mesh):
    return jax.shard_map(
        shards,
        mesh=mesh,
        in_specs=(
            P("parts", None, "scan", None),
            P("parts", None, None, None),
            P(),
            P(("parts", "scan"), None, None),
            P(("parts", "scan"), None),
            P(("parts", "scan")),
        ),
        out_specs=(
            P("parts", None, "scan", None),
            P("parts", None, None, None),
            P(("parts", "scan")),
        ),
        check_vma=False,
    )
```

profile of v0, /device:TPU:0, one launch (start us, length us, event | category | flops | bytes accessed | tf_op | source)
XLA Modules:
  0.0 100.9 jit_solution(14929372471703015789)
XLA Ops:
  0.6 0.5 collective-permute-start
  1.8 1.9 %shard_map.94.refs_3_.packed.refs_5_ = f32[1032,128]{1,0:T(8,128)} custom-call(s32[2,8]{1,0:T(2,128)} %bitcast.14, s32[1]{0:T(128)S(6)} %copy.10.live, f32[1024,128]{1,0:T(8,128)} %bitcast.12), custom_call_target="tpu_custom_call" | custom-call | tf_op jit(solution)/shard_map/pallas_call | solution.py:87
  3.8 5.7 %collective-permute-start.2 = (f32[1032,128]{1,0:T(8,128)}, f32[1032,128]{1,0:T(8,128)}, u32[]{:S(2)}, u32[]{:S(2)}) collective-permute-start(f32[1032,128]{1,0:T(8,128)} %shard_map.94.refs_3_.packed.refs_5_), channel_id=1, source_target_pairs={{0,2},{1,3},{2,4},{3,5},{4,6},{5,7},{6,8},{7,9},{8,10},{9,11},{10,... | collective-permute-start | bytes 1585160 | tf_op jit(solution)/shard_map/ppermute | solution.py:24
  9.4 0.6 pad_add_fusion.refs_0_.place
  10.1 1.0 copy-done.2
  11.1 3.2 %shard_map.96 = f32[1544,128]{1,0:T(8,128)} custom-call(s32[3]{0:T(128)} %pad_add_fusion.refs_0_.place, f32[1032,128]{1,0:T(8,128)} %shard_map.94.refs_3_.packed.refs_5_, f32[2,2,256,256]{3,2,1,0:T(8,128)} %refs_1_.3, f32[2,2,256,256]{3,2,1,0:T(8,128)} %copy-done.2), custom_call_target="tpu_custom_call" | custom-call | tf_op jit(solution)/shard_map/pallas_call | solution.py:97
  14.3 1.3 %collective-permute-start.3 = (f32[1544,128]{1,0:T(8,128)}, f32[1544,128]{1,0:T(8,128)S(1)}, u32[]{:S(2)}, u32[]{:S(2)}) collective-permute-start(f32[1544,128]{1,0:T(8,128)} %shard_map.96), channel_id=1, source_target_pairs={{2,0},{3,1},{4,2},{5,3},{6,4},{7,5},{8,6},{9,7},{10,8},{11,9},{12,... | collective-permute-start | bytes 2371592 | tf_op jit(solution)/shard_map/ppermute | solution.py:24
  15.6 0.2 cosine_bitcast_fusion
  16.0 1.2 %copy-done.3 = f32[2,2,256,256]{3,2,1,0:T(8,128)S(1)} copy-done((f32[2,2,256,256]{3,2,1,0:T(8,128)S(1)}, f32[2,2,256,256]{3,2,1,0:T(8,128)}, u32[]{:S(2)}) %copy-start.3) | copy-done | bytes 1048600
  17.2 1.0 %copy-done.5 = f32[4,2,128,128]{3,2,1,0:T(8,128)S(1)} copy-done((f32[4,2,128,128]{3,2,1,0:T(8,128)S(1)}, f32[4,2,128,128]{3,2,1,0:T(8,128)}, u32[]{:S(2)}) %copy-start.5) | copy-done | bytes 524312
  18.2 16.3 %shard_map.95 = (f32[2,2,512,256]{3,2,1,0:T(8,128)}, f32[1056,128]{1,0:T(8,128)S(1)}) custom-call(s32[3]{0:T(128)S(1)} %copy-done.4, f32[2,2,256,256]{3,2,1,0:T(8,128)S(1)} %copy-done.1, f32[2,2,256,256]{3,2,1,0:T(8,128)S(1)} %copy-done.3, f32[1032,128]{1,0:T(8,128)S(1)} %copy-done, f32[1032,128]{1,0:T(8,128)S(1)} %collective-permute-done.1.refs_4_.refs_6_, ...), custom_call_target="tpu_custom_call" | custom-call | flops 4831838208 | bytes 8388608 | tf_op jit(solution)/shard_map/pallas_call | solution.py:407
  34.5 2.8 %collective-permute-done.2.refs_3_ = f32[1032,128]{1,0:T(8,128)} collective-permute-done((f32[1032,128]{1,0:T(8,128)}, f32[1032,128]{1,0:T(8,128)}, u32[]{:S(2)}, u32[]{:S(2)}) %collective-permute-start.2) | collective-permute-done | bytes 528416 | tf_op jit(solution)/shard_map/ppermute | solution.py:24
  37.3 0.5 collective-permute-start.4
  37.8 2.4 %collective-permute-done.4.refs_4_ = f32[1032,128]{1,0:T(8,128)S(1)} collective-permute-done((f32[1032,128]{1,0:T(8,128)}, f32[1032,128]{1,0:T(8,128)S(1)}, u32[]{:S(2)}, u32[]{:S(2)}) %collective-permute-start.4) | collective-permute-done | bytes 528416 | tf_op jit(solution)/shard_map/ppermute | solution.py:29
  40.2 0.1 collective-permute-done.5.refs_8_
  40.4 15.7 %shard_map.97 = (f32[2,2,256,256]{3,2,1,0:T(8,128)}, f32[2,2,384,256]{3,2,1,0:T(8,128)}, f32[1056,128]{1,0:T(8,128)S(1)}) custom-call(s32[3]{0:T(128)S(1)} %copy-done.4, f32[2,2,256,256]{3,2,1,0:T(8,128)} %refs_1_.3, f32[2,2,256,256]{3,2,1,0:T(8,128)} %copy-done.2, f32[1032,128]{1,0:T(8,128)} %collective-permute-done.2.refs_3_, ...), custom_call_target="tpu_custom_call" | custom-call | flops 4831838208 | bytes 8388608 | tf_op jit(solution)/shard_map/pallas_call | solution.py:407
  56.1 0.3 collective-permute-start.8
  56.4 0.4 collective-permute-start.6
  56.8 3.2 %collective-permute-done.6 = f32[528,128]{1,0:T(8,128)S(1)} collective-permute-done((f32[528,128]{1,0:T(8,128)S(1)}, f32[528,128]{1,0:T(8,128)S(1)}, u32[]{:S(2)}, u32[]{:S(2)}) %collective-permute-start.6) | collective-permute-done | bytes 270368 | tf_op jit(solution)/shard_map/ppermute | solution.py:29
  60.0 4.4 %collective-permute-start.7 = (f32[264,128]{1,0:T(8,128)S(1)}, f32[264,128]{1,0:T(8,128)S(1)}, u32[]{:S(2)}, u32[]{:S(2)}) collective-permute-start(f32[264,128]{1,0:T(8,128)S(1)} %constant_dynamic-slice_fusion), channel_id=1, source_target_pairs={{0,2},{1,3},{2,0},{3,1},{4,6},{5,7},{6,4},{7,5},{8,10},{9,11},{10,... | collective-permute-start | bytes 405512 | tf_op jit(solution)/shard_map/ppermute | solution.py:29
  64.4 1.1 %slice_add_fusion.1 = f32[2,2,128,256]{3,2,1,0:T(8,128)S(1)} fusion(f32[2,2,384,256]{3,2,1,0:T(8,128)S(1)} %collective-permute-done.8, f32[2,2,384,256]{3,2,1,0:T(8,128)} %get-tuple-element.25), kind=kLoop, calls=%fused_computation.2 | loop fusion | flops 131072 | bytes 1572864 | tf_op jit(solution)/shard_map/add | solution.py:461
  65.5 2.9 %collective-permute-done.7 = f32[264,128]{1,0:T(8,128)S(1)} collective-permute-done((f32[264,128]{1,0:T(8,128)S(1)}, f32[264,128]{1,0:T(8,128)S(1)}, u32[]{:S(2)}, u32[]{:S(2)}) %collective-permute-start.7) | collective-permute-done | bytes 135200 | tf_op jit(solution)/shard_map/ppermute | solution.py:29
  68.4 0.7 collective-permute-start.11
  69.2 5.0 %collective-permute-done.9 = f32[264,128]{1,0:T(8,128)S(1)} collective-permute-done((f32[264,128]{1,0:T(8,128)S(1)}, f32[264,128]{1,0:T(8,128)S(1)}, u32[]{:S(2)}, u32[]{:S(2)}) %collective-permute-start.9) | collective-permute-done | bytes 135200 | tf_op jit(solution)/shard_map/ppermute | solution.py:29
  74.2 10.9 %collective-permute-start.10 = (f32[264,128]{1,0:T(8,128)S(1)}, f32[264,128]{1,0:T(8,128)S(1)}, u32[]{:S(2)}, u32[]{:S(2)}) collective-permute-start(f32[264,128]{1,0:T(8,128)S(1)} %add.60), channel_id=1, source_target_pairs={{0,8},{1,9},{2,10},{3,11},{4,12},{5,13},{6,14},{7,15},{8,0},{9,1},... | collective-permute-start | bytes 405512 | tf_op jit(solution)/shard_map/ppermute | solution.py:29
  85.1 2.4 %fusion = f32[2,2,256,256]{3,2,1,0:T(8,128)} fusion(f32[2,2,256,256]{3,2,1,0:T(8,128)} %get-tuple-element.27, f32[2,2,384,256]{3,2,1,0:T(8,128)S(1)} %collective-permute-done.8, f32[2,2,128,256]{3,2,1,0:T(8,128)S(1)} %collective-permute-done.11), kind=kLoop, calls=%fused_computation.1 | loop fusion | flops 524288 | bytes 3670016 | tf_op jit(solution)/shard_map/add | solution.py:466
  87.5 4.4 %collective-permute-done.10 = f32[264,128]{1,0:T(8,128)S(1)} collective-permute-done((f32[264,128]{1,0:T(8,128)S(1)}, f32[264,128]{1,0:T(8,128)S(1)}, u32[]{:S(2)}, u32[]{:S(2)}) %collective-permute-start.10) | collective-permute-done | bytes 135200 | tf_op jit(solution)/shard_map/ppermute | solution.py:29
  92.0 6.4 %collective-permute-done.12 = f32[264,128]{1,0:T(8,128)S(1)} collective-permute-done((f32[264,128]{1,0:T(8,128)S(1)}, f32[264,128]{1,0:T(8,128)S(1)}, u32[]{:S(2)}, u32[]{:S(2)}) %collective-permute-start.12) | collective-permute-done | bytes 135200 | tf_op jit(solution)/shard_map/ppermute | solution.py:29
  98.4 0.1 collective-permute-start.13
  98.5 0.6 dynamic_slice.19
  99.1 0.9 collective-permute-done.13
  100.1 0.8 pad_maximum_fusion
  (35 shorter events, 0.5 us)
Async XLA Ops:
  0.6 9.5 %collective-permute-start = (f32[2,2,256,256]{3,2,1,0:T(8,128)}, f32[2,2,256,256]{3,2,1,0:T(8,128)S(1)}, u32[]{:S(2)}, u32[]{:S(2)}) collective-permute-start(f32[2,2,256,256]{3,2,1,0:T(8,128)} %refs_1_.3), channel_id=1, source_target_pairs={{0,1},{1,0},{2,3},{3,2},{4,5},{5,4},{6,7},{7,6},{8,9},{9,8},{10,11... | collective-permute-start | bytes 3145736 | tf_op jit(solution)/shard_map/ppermute | solution.py:29
  3.7 12.2 %collective-permute-start.1 = (f32[1032,128]{1,0:T(8,128)}, f32[1032,128]{1,0:T(8,128)S(1)}, u32[]{:S(2)}, u32[]{:S(2)}) collective-permute-start(f32[1032,128]{1,0:T(8,128)} %shard_map.94.refs_3_.packed.refs_5_), channel_id=1, source_target_pairs={{0,1},{1,0},{2,3},{3,2},{4,5},{5,4},{6,7},{7,6},{8,9},{9,8},{10,11... | collective-permute-start | bytes 1585160 | tf_op jit(solution)/shard_map/ppermute | solution.py:29
  3.8 33.6 %collective-permute-start.2 = (f32[1032,128]{1,0:T(8,128)}, f32[1032,128]{1,0:T(8,128)}, u32[]{:S(2)}, u32[]{:S(2)}) collective-permute-start(f32[1032,128]{1,0:T(8,128)} %shard_map.94.refs_3_.packed.refs_5_), channel_id=1, source_target_pairs={{0,2},{1,3},{2,4},{3,5},{4,6},{5,7},{6,8},{7,9},{8,10},{9,11},{10,... | collective-permute-start | bytes 1585160 | tf_op jit(solution)/shard_map/ppermute | solution.py:24
  10.1 5.5 %copy-start.8 = (f32[128,128]{1,0:T(8,128)S(1)}, f32[128,128]{1,0:T(8,128)}, u32[]{:S(2)}) copy-start(f32[128,128]{1,0:T(8,128)} %param.9) | copy-start | bytes 196612
  10.1 5.8 %copy-start = (f32[1032,128]{1,0:T(8,128)S(1)}, f32[1032,128]{1,0:T(8,128)}, u32[]{:S(2)}) copy-start(f32[1032,128]{1,0:T(8,128)} %shard_map.94.refs_3_.packed.refs_5_) | copy-start | bytes 1585156
  10.1 5.8 %copy-start.1 = (f32[2,2,256,256]{3,2,1,0:T(8,128)S(1)}, f32[2,2,256,256]{3,2,1,0:T(8,128)}, u32[]{:S(2)}) copy-start(f32[2,2,256,256]{3,2,1,0:T(8,128)} %refs_1_.3) | copy-start | bytes 3145732
  10.1 5.8 %copy-start.4 = (s32[3]{0:T(128)S(1)}, s32[3]{0:T(128)}, u32[]{:S(2)}) copy-start(s32[3]{0:T(128)} %pad_add_fusion.refs_0_.place) | copy-start | bytes 40
  10.1 5.9 %copy-start.7 = (f32[2,128,128]{2,1,0:T(8,128)S(1)}, f32[2,128,128]{2,1,0:T(8,128)}, u32[]{:S(2)}) copy-start(f32[2,128,128]{2,1,0:T(8,128)} %constant.76.clone.refs_7_.refs_13_) | copy-start | bytes 393220
  10.1 1.0 copy-start.2
  14.3 23.0 %collective-permute-start.3 = (f32[1544,128]{1,0:T(8,128)}, f32[1544,128]{1,0:T(8,128)S(1)}, u32[]{:S(2)}, u32[]{:S(2)}) collective-permute-start(f32[1544,128]{1,0:T(8,128)} %shard_map.96), channel_id=1, source_target_pairs={{2,0},{3,1},{4,2},{5,3},{6,4},{7,5},{8,6},{9,7},{10,8},{11,9},{12,... | collective-permute-start | bytes 2371592 | tf_op jit(solution)/shard_map/ppermute | solution.py:24
  15.9 1.2 %copy-start.3 = (f32[2,2,256,256]{3,2,1,0:T(8,128)S(1)}, f32[2,2,256,256]{3,2,1,0:T(8,128)}, u32[]{:S(2)}) copy-start(f32[2,2,256,256]{3,2,1,0:T(8,128)} %copy-done.2) | copy-start | bytes 3145732
  17.2 1.0 %copy-start.5 = (f32[4,2,128,128]{3,2,1,0:T(8,128)S(1)}, f32[4,2,128,128]{3,2,1,0:T(8,128)}, u32[]{:S(2)}) copy-start(f32[4,2,128,128]{3,2,1,0:T(8,128)} %refs_11_.1) | copy-start | bytes 1572868
  18.2 22.1 %copy-start.6 = (f32[4,2,128,128]{3,2,1,0:T(8,128)S(1)}, f32[4,2,128,128]{3,2,1,0:T(8,128)}, u32[]{:S(2)}) copy-start(f32[4,2,128,128]{3,2,1,0:T(8,128)} %refs_11_.1) | copy-start | bytes 1572868
  37.3 3.0 %collective-permute-start.5 = (f32[1544,128]{1,0:T(8,128)S(1)}, f32[1544,128]{1,0:T(8,128)S(1)}, u32[]{:S(2)}, u32[]{:S(2)}) collective-permute-start(f32[1544,128]{1,0:T(8,128)S(1)} %collective-permute-done.3.refs_7_), channel_id=1, source_target_pairs={{0,1},{1,0},{2,3},{3,2},{4,5},{5,4},{6,7},{7,6},{8,9},{9,8},{10,11... | collective-permute-start | bytes 2371592 | tf_op jit(solution)/shard_map/ppermute | solution.py:29
  37.3 2.9 %collective-permute-start.4 = (f32[1032,128]{1,0:T(8,128)}, f32[1032,128]{1,0:T(8,128)S(1)}, u32[]{:S(2)}, u32[]{:S(2)}) collective-permute-start(f32[1032,128]{1,0:T(8,128)} %collective-permute-done.2.refs_3_), channel_id=1, source_target_pairs={{0,1},{1,0},{2,3},{3,2},{4,5},{5,4},{6,7},{7,6},{8,9},{9,8},{10,11... | collective-permute-start | bytes 1585160 | tf_op jit(solution)/shard_map/ppermute | solution.py:29
  56.1 8.3 %collective-permute-start.8 = (f32[2,2,384,256]{3,2,1,0:T(8,128)}, f32[2,2,384,256]{3,2,1,0:T(8,128)S(1)}, u32[]{:S(2)}, u32[]{:S(2)}) collective-permute-start(f32[2,2,384,256]{3,2,1,0:T(8,128)} %get-tuple-element.25), channel_id=1, source_target_pairs={{0,1},{1,0},{2,3},{3,2},{4,5},{5,4},{6,7},{7,6},{8,9},{9,8},{10,11... | collective-permute-start | bytes 4718600 | tf_op jit(solution)/shard_map/ppermute | solution.py:29
  56.4 3.6 %collective-permute-start.6 = (f32[528,128]{1,0:T(8,128)S(1)}, f32[528,128]{1,0:T(8,128)S(1)}, u32[]{:S(2)}, u32[]{:S(2)}) collective-permute-start(f32[528,128]{1,0:T(8,128)S(1)} %constant_dynamic-slice_fusion.1), channel_id=1, source_target_pairs={{0,1},{1,0},{2,3},{3,2},{4,5},{5,4},{6,7},{7,6},{8,9},{9,8},{10,11... | collective-permute-start | bytes 811016 | tf_op jit(solution)/shard_map/ppermute | solution.py:29
  60.0 8.4 %collective-permute-start.7 = (f32[264,128]{1,0:T(8,128)S(1)}, f32[264,128]{1,0:T(8,128)S(1)}, u32[]{:S(2)}, u32[]{:S(2)}) collective-permute-start(f32[264,128]{1,0:T(8,128)S(1)} %constant_dynamic-slice_fusion), channel_id=1, source_target_pairs={{0,2},{1,3},{2,0},{3,1},{4,6},{5,7},{6,4},{7,5},{8,10},{9,11},{10,... | collective-permute-start | bytes 405512 | tf_op jit(solution)/shard_map/ppermute | solution.py:29
  68.4 16.7 %collective-permute-start.11 = (f32[2,2,128,256]{3,2,1,0:T(8,128)S(1)}, f32[2,2,128,256]{3,2,1,0:T(8,128)S(1)}, u32[]{:S(2)}, u32[]{:S(2)}) collective-permute-start(f32[2,2,128,256]{3,2,1,0:T(8,128)S(1)} %slice_add_fusion.1), channel_id=1, source_target_pairs={{1,2},{3,4},{5,6},{7,8},{9,10},{11,12},{13,14},{17,18},{19,20},{21... | collective-permute-start | bytes 1572872 | tf_op jit(solution)/shard_map/ppermute | solution.py:465
  69.1 5.1 %collective-permute-start.9 = (f32[264,128]{1,0:T(8,128)S(1)}, f32[264,128]{1,0:T(8,128)S(1)}, u32[]{:S(2)}, u32[]{:S(2)}) collective-permute-start(f32[264,128]{1,0:T(8,128)S(1)} %dynamic-slice_add_fusion.1), channel_id=1, source_target_pairs={{0,4},{1,5},{2,6},{3,7},{4,0},{5,1},{6,2},{7,3},{8,12},{9,13},{10,... | collective-permute-start | bytes 405512 | tf_op jit(solution)/shard_map/ppermute | solution.py:29
  74.2 17.7 %collective-permute-start.10 = (f32[264,128]{1,0:T(8,128)S(1)}, f32[264,128]{1,0:T(8,128)S(1)}, u32[]{:S(2)}, u32[]{:S(2)}) collective-permute-start(f32[264,128]{1,0:T(8,128)S(1)} %add.60), channel_id=1, source_target_pairs={{0,8},{1,9},{2,10},{3,11},{4,12},{5,13},{6,14},{7,15},{8,0},{9,1},... | collective-permute-start | bytes 405512 | tf_op jit(solution)/shard_map/ppermute | solution.py:29
  91.9 6.4 %collective-permute-start.12 = (f32[264,128]{1,0:T(8,128)S(1)}, f32[264,128]{1,0:T(8,128)S(1)}, u32[]{:S(2)}, u32[]{:S(2)}) collective-permute-start(f32[264,128]{1,0:T(8,128)S(1)} %add.63), channel_id=1, source_target_pairs={{0,2},{1,3},{2,0},{3,1},{4,6},{5,7},{6,4},{7,5},{8,10},{9,11},{10,... | collective-permute-start | bytes 405512 | tf_op jit(solution)/shard_map/ppermute | solution.py:29
  98.4 1.6 %collective-permute-start.13 = (f32[512,128]{1,0:T(8,128)S(1)}, f32[512,128]{1,0:T(8,128)S(1)}, u32[]{:S(2)}, u32[]{:S(2)}) collective-permute-start(f32[512,128]{1,0:T(8,128)S(1)} %pad_maximum_fusion.1), channel_id=1, source_target_pairs={{0,1},{1,0},{2,3},{3,2},{4,5},{5,4},{6,7},{7,6},{8,9},{9,8},{10,11... | collective-permute-start | bytes 786440 | tf_op jit(solution)/shard_map/ppermute | solution.py:29
where the time goes:
time: 100 us; the launch traced here: 101 us
  Pallas kernels  37.2 us (37%)
  waiting for transfers between devices  28 us (28%)
  starting transfers between devices  24.9 us (25%)
  other arithmetic  5.17 us (5%)
  local copies, waits for them, and re-layouts  4.11 us (4%)
  between operations  1.5 us (2%)
    pallas_call x2, Pallas kernels, windows(): pl.pallas_call(functools.partial(flat_kernel, early, size, modes, slots,...  32 us
    ppermute x11, waiting for transfers between devices, swapped(): lax.ppermute(value, axis, [(source, source ^ bit) for source in range(cou...  25.3 us
    ppermute x11, starting transfers between devices, swapped(): lax.ppermute(value, axis, [(source, source ^ bit) for source in range(cou...  17.3 us
    ppermute x2, starting transfers between devices, shifted(): lax.ppermute(value, axis, [(source, source + steps) for source in range(f...  6.96 us
    unnamed x18, local copies, waits for them, and re-layouts  3.25 us
    pallas_call x1, Pallas kernels, add_halo(): pl.pallas_call(add_halo_kernel, out_shape=jax.ShapeDtypeStruct((rows + 4...  3.23 us
    ppermute x2, waiting for transfers between devices, shifted(): lax.ppermute(value, axis, [(source, source + steps) for source in range(f...  2.77 us
    add x1, other arithmetic, shards(): mine + back[:, :, :tile]  2.37 us
  transfers between devices with their start and end apart: 14, of which 9 were waited for; matrix products, arithmetic and copies ran while one was open for 5% of the time, Pallas kernels for 21%

commit v1 on v0

--- a/solution.py
+++ b/solution.py
@@ -139,10 +139,8 @@
                     far_off = pl.multiple_of(2 * tile + half - core * half, half)
                     move(packs[4].at[block], obj.at[k, ri, pl.ds(near, half), lanes])
                     move(packs[5].at[block], obj.at[k, ri, pl.ds(far_off, half), lanes])
-        old_grad, old_sums = before
-        move(old_grad, acc.at[:, :, pl.ds(0, 2 * tile)])
-        move(old_sums, sums_ref)
-        acc[:, :, 2 * tile:] = jnp.zeros((2, 2, size, acc.shape[3]), F32)
+        move(before[0], sums_ref)
+        acc[...] = jnp.zeros_like(acc)
 
     right_f, right_g, left_f, left_g = (tables.at[i] for i in range(4))
     cosine, sine = table_ref[0], table_ref[1]
@@ -357,7 +355,9 @@
         together([(0, number - 1)])
 
     if early:
-        move(acc.at[:, :, pl.ds(0, 2 * tile)], outs[0])
+        mine_ref, theirs_ref = outs
+        move(acc.at[:, :, pl.ds(top, tile)], mine_ref)
+        move(acc.at[:, :, pl.ds(other, tile)], theirs_ref)
     else:
         mine_ref, theirs_ref = outs
         move(acc.at[:, :, pl.ds(top, tile)], mine_ref)
@@ -381,7 +381,7 @@
     early = not before
     sums = jax.ShapeDtypeStruct((2 * modes * size + 2 * LOSS_PAD, size), F32)
     if early:
-        outs = (jax.ShapeDtypeStruct((2, 2, 2 * tile, columns), F32),)
+        outs = (jax.ShapeDtypeStruct((2, 2, tile, columns), F32),) * 2
     else:
         outs = (
             jax.ShapeDtypeStruct((2, 2, tile, columns), F32),
@@ -450,10 +450,11 @@
     pair_packed = swapped(packed, "scan", 1)
     down = shifted(add_halo(place, packed, object_slices, pair), "scan", -2)
     shared = (probe_modes, prop, table, slots)
-    before = windows(place, object_slices, pair, (packed, pair_packed), (), *shared)
-    before, up, down = lax.optimization_barrier((before, up, down))
+    first_mine, first_theirs, first_sums = windows(place, object_slices, pair, (packed, pair_packed), (), *shared)
+    first_theirs, first_sums, up, down = lax.optimization_barrier((first_theirs, first_sums, up, down))
+    first_back = swapped(first_theirs, "scan", 1)
     packs = (up, swapped(up, "scan", 1), packed, pair_packed, down, swapped(down, "scan", 1))
-    mine, theirs, sums = windows(place, object_slices, pair, packs, before, *shared)
+    mine, theirs, sums = windows(place, object_slices, pair, packs, (first_sums,), *shared)
 
     kept, given = halves(sums, "scan", 1)
     sums = kept + swapped(given, "scan", 1)
@@ -463,7 +464,7 @@
     got, halo = swapped_beside(given, "scan", 2, halo)
     sums = kept + got
     halo = lax.ppermute(halo, "scan", [(s, s + 1) for s in range(1, count - 1, 2)])
-    grad = mine + back[:, :, :tile] + jnp.pad(halo, ((0, 0), (0, 0), (0, tile - size), (0, 0)))
+    grad = first_mine + first_back + mine + back[:, :, :tile] + jnp.pad(halo, ((0, 0), (0, 0), (0, tile - size), (0, 0)))
     bit = 4
     while bit < count:
         if 2 * bit < count:

time: 100 us -> 102 us (1.020)
  the two profiles are of different devices: /device:TPU:0 before, /device:TPU:18 now
where the time goes in v1:
time: 102 us
  waiting for transfers between devices  32.6 us (32%)
  starting transfers between devices  28.4 us (28%)
  Pallas kernels  27.6 us (27%)
  other arithmetic  6.28 us (6%)
  local copies, waits for them, and re-layouts  5.75 us (6%)
  between operations  1.54 us (2%)
    pallas_call x2, Pallas kernels, windows(): pl.pallas_call(functools.partial(flat_kernel, early, size, modes, slots,...  22.4 us
    ppermute x12, waiting for transfers between devices, swapped(): lax.ppermute(value, axis, [(source, source ^ bit) for source in range(cou...  21.7 us
    ppermute x12, starting transfers between devices, swapped(): lax.ppermute(value, axis, [(source, source ^ bit) for source in range(cou...  20.4 us
    ppermute x2, waiting for transfers between devices, shifted(): lax.ppermute(value, axis, [(source, source + steps) for source in range(f...  10.9 us
    ppermute x2, starting transfers between devices, shifted(): lax.ppermute(value, axis, [(source, source + steps) for source in range(f...  6.73 us
    unnamed x24, local copies, waits for them, and re-layouts  4.88 us
    add x1, other arithmetic, shards(): first_mine + first_back + mine + back[:, :, :tile]  3.3 us
    pallas_call x1, Pallas kernels, add_halo(): pl.pallas_call(add_halo_kernel, out_shape=jax.ShapeDtypeStruct((rows + 4...  3.24 us
  transfers between devices with their start and end apart: 15, of which 9 were waited for; matrix products, arithmetic and copies ran while one was open for 6% of the time, Pallas kernels for 12%

profile of v1, /device:TPU:18, one launch (start us, length us, event | category | flops | bytes accessed | tf_op | source)
XLA Modules:
  0.0 102.2 jit_solution(304732765820424084)
XLA Ops:
  1.4 1.9 %shard_map.94.refs_3_.packed.refs_5_ = f32[1032,128]{1,0:T(8,128)} custom-call(s32[2,8]{1,0:T(2,128)} %bitcast.14, s32[1]{0:T(128)S(6)} %copy.10.live, f32[1024,128]{1,0:T(8,128)} %bitcast.12), custom_call_target="tpu_custom_call" | custom-call | tf_op jit(solution)/shard_map/pallas_call | solution.py:87
  3.3 0.5 collective-permute-start.1
  3.8 3.4 %collective-permute-start.2 = (f32[1032,128]{1,0:T(8,128)}, f32[1032,128]{1,0:T(8,128)}, u32[]{:S(2)}, u32[]{:S(2)}) collective-permute-start(f32[1032,128]{1,0:T(8,128)} %shard_map.94.refs_3_.packed.refs_5_), channel_id=1, source_target_pairs={{0,2},{1,3},{2,4},{3,5},{4,6},{5,7},{6,8},{7,9},{8,10},{9,11},{10,... | collective-permute-start | bytes 1585160 | tf_op jit(solution)/shard_map/ppermute | solution.py:24
  7.2 0.7 pad_add_fusion.refs_0_.place
  7.9 1.0 copy-done.10
  8.9 3.2 %shard_map.96 = f32[1544,128]{1,0:T(8,128)} custom-call(s32[3]{0:T(128)} %pad_add_fusion.refs_0_.place, f32[1032,128]{1,0:T(8,128)} %shard_map.94.refs_3_.packed.refs_5_, f32[2,2,256,256]{3,2,1,0:T(8,128)} %refs_1_.3, f32[2,2,256,256]{3,2,1,0:T(8,128)} %copy-done.10), custom_call_target="tpu_custom_call" | custom-call | tf_op jit(solution)/shard_map/pallas_call | solution.py:97
  12.1 3.3 %collective-permute-start.3 = (f32[1544,128]{1,0:T(8,128)}, f32[1544,128]{1,0:T(8,128)S(1)}, u32[]{:S(2)}, u32[]{:S(2)}) collective-permute-start(f32[1544,128]{1,0:T(8,128)} %shard_map.96), channel_id=1, source_target_pairs={{2,0},{3,1},{4,2},{5,3},{6,4},{7,5},{8,6},{9,7},{10,8},{11,9},{12,... | collective-permute-start | bytes 2371592 | tf_op jit(solution)/shard_map/ppermute | solution.py:24
  15.8 0.8 copy-done.5
  16.6 1.0 %copy-done.6 = f32[1032,128]{1,0:T(8,128)S(1)} copy-done((f32[1032,128]{1,0:T(8,128)S(1)}, f32[1032,128]{1,0:T(8,128)}, u32[]{:S(2)}) %copy-start.6) | copy-done | bytes 528408
  17.6 1.0 %copy-done.7 = f32[4,2,128,128]{3,2,1,0:T(8,128)S(1)} copy-done((f32[4,2,128,128]{3,2,1,0:T(8,128)S(1)}, f32[4,2,128,128]{3,2,1,0:T(8,128)}, u32[]{:S(2)}) %copy-start.7) | copy-done | bytes 524312
  18.7 7.1 %shard_map.95 = (f32[2,2,256,256]{3,2,1,0:T(8,128)S(1)}, f32[2,2,256,256]{3,2,1,0:T(8,128)S(1)}, f32[1056,128]{1,0:T(8,128)S(1)}) custom-call(s32[3]{0:T(128)S(1)} %copy-done.2, f32[2,2,256,256]{3,2,1,0:T(8,128)S(1)} %copy-done.1, f32[2,2,256,256]{3,2,1,0:T(8,128)} %copy-done.10, f32[1032,128]{1,0:T(8,128)S(1)} %copy-done, f32[1032,128]{1,0:T(8,128)S(1)} %copy-done.6, ...), custom_call_target="tpu_custom_call" | custom-call | flops 4831838208 | bytes 8388608 | tf_op jit(solution)/shard_map/pallas_call | solution.py:407
  25.7 1.0 copy-done.3
  26.8 9.1 %collective-permute-done.2.refs_3_ = f32[1032,128]{1,0:T(8,128)} collective-permute-done((f32[1032,128]{1,0:T(8,128)}, f32[1032,128]{1,0:T(8,128)}, u32[]{:S(2)}, u32[]{:S(2)}) %collective-permute-start.2) | collective-permute-done | bytes 528416 | tf_op jit(solution)/shard_map/ppermute | solution.py:24
  35.9 1.8 %collective-permute-done.3.refs_7_ = f32[1544,128]{1,0:T(8,128)S(1)} collective-permute-done((f32[1544,128]{1,0:T(8,128)}, f32[1544,128]{1,0:T(8,128)S(1)}, u32[]{:S(2)}, u32[]{:S(2)}) %collective-permute-start.3) | collective-permute-done | bytes 790560 | tf_op jit(solution)/shard_map/ppermute | solution.py:24
  37.6 0.5 collective-permute-start.4
  38.1 2.5 %collective-permute-done.4.refs_4_ = f32[1032,128]{1,0:T(8,128)S(1)} collective-permute-done((f32[1032,128]{1,0:T(8,128)}, f32[1032,128]{1,0:T(8,128)S(1)}, u32[]{:S(2)}, u32[]{:S(2)}) %collective-permute-start.4) | collective-permute-done | bytes 528416 | tf_op jit(solution)/shard_map/ppermute | solution.py:29
  40.7 15.4 %shard_map.97 = (f32[2,2,256,256]{3,2,1,0:T(8,128)}, f32[2,2,384,256]{3,2,1,0:T(8,128)}, f32[1056,128]{1,0:T(8,128)S(1)}) custom-call(s32[3]{0:T(128)S(1)} %copy-done.2, f32[2,2,256,256]{3,2,1,0:T(8,128)} %refs_1_.3, f32[2,2,256,256]{3,2,1,0:T(8,128)} %copy-done.10, f32[1032,128]{1,0:T(8,128)} %collective-permute-done.2.refs_3_, ...), custom_call_target="tpu_custom_call" | custom-call | flops 4831838208 | bytes 8388608 | tf_op jit(solution)/shard_map/pallas_call | solution.py:407
  56.4 0.4 collective-permute-start.6
  57.0 3.4 %collective-permute-done.6 = f32[528,128]{1,0:T(8,128)S(1)} collective-permute-done((f32[528,128]{1,0:T(8,128)S(1)}, f32[528,128]{1,0:T(8,128)S(1)}, u32[]{:S(2)}, u32[]{:S(2)}) %collective-permute-start.6) | collective-permute-done | bytes 270368 | tf_op jit(solution)/shard_map/ppermute | solution.py:29
  60.4 2.5 %collective-permute-start.7 = (f32[264,128]{1,0:T(8,128)S(1)}, f32[264,128]{1,0:T(8,128)S(1)}, u32[]{:S(2)}, u32[]{:S(2)}) collective-permute-start(f32[264,128]{1,0:T(8,128)S(1)} %constant_dynamic-slice_fusion), channel_id=1, source_target_pairs={{0,2},{1,3},{2,0},{3,1},{4,6},{5,7},{6,4},{7,5},{8,10},{9,11},{10,... | collective-permute-start | bytes 405512 | tf_op jit(solution)/shard_map/ppermute | solution.py:29
  62.9 1.3 %slice_add_fusion.1 = f32[2,2,128,256]{3,2,1,0:T(8,128)S(1)} fusion(f32[2,2,384,256]{3,2,1,0:T(8,128)} %collective-permute-done.8, f32[2,2,384,256]{3,2,1,0:T(8,128)} %get-tuple-element.25), kind=kLoop, calls=%fused_computation.2 | loop fusion | flops 131072 | bytes 1572864 | tf_op jit(solution)/shard_map/add | solution.py:462
  64.1 2.8 %collective-permute-done.7 = f32[264,128]{1,0:T(8,128)S(1)} collective-permute-done((f32[264,128]{1,0:T(8,128)S(1)}, f32[264,128]{1,0:T(8,128)S(1)}, u32[]{:S(2)}, u32[]{:S(2)}) %collective-permute-start.7) | collective-permute-done | bytes 135200 | tf_op jit(solution)/shard_map/ppermute | solution.py:29
  67.0 1.3 %collective-permute-start.12 = (f32[2,2,128,256]{3,2,1,0:T(8,128)S(1)}, f32[2,2,128,256]{3,2,1,0:T(8,128)}, u32[]{:S(2)}, u32[]{:S(2)}) collective-permute-start(f32[2,2,128,256]{3,2,1,0:T(8,128)S(1)} %slice_add_fusion.1), channel_id=1, source_target_pairs={{1,2},{3,4},{5,6},{7,8},{9,10},{11,12},{13,14},{17,18},{19,20},{21... | collective-permute-start | bytes 1572872 | tf_op jit(solution)/shard_map/ppermute | solution.py:466
  68.3 13.1 %collective-permute-start.9 = (f32[264,128]{1,0:T(8,128)S(1)}, f32[264,128]{1,0:T(8,128)S(1)}, u32[]{:S(2)}, u32[]{:S(2)}) collective-permute-start(f32[264,128]{1,0:T(8,128)S(1)} %dynamic-slice_add_fusion.1), channel_id=1, source_target_pairs={{0,4},{1,5},{2,6},{3,7},{4,0},{5,1},{6,2},{7,3},{8,12},{9,13},{10,... | collective-permute-start | bytes 405512 | tf_op jit(solution)/shard_map/ppermute | solution.py:29
  81.4 3.3 %collective-permute-done.9 = f32[264,128]{1,0:T(8,128)S(1)} collective-permute-done((f32[264,128]{1,0:T(8,128)S(1)}, f32[264,128]{1,0:T(8,128)S(1)}, u32[]{:S(2)}, u32[]{:S(2)}) %collective-permute-start.9) | collective-permute-done | bytes 135200 | tf_op jit(solution)/shard_map/ppermute | solution.py:29
  84.8 3.3 %fusion = f32[2,2,256,256]{3,2,1,0:T(8,128)} fusion(f32[2,2,384,256]{3,2,1,0:T(8,128)} %collective-permute-done.8, f32[2,2,128,256]{3,2,1,0:T(8,128)} %collective-permute-done.12, f32[2,2,256,256]{3,2,1,0:T(8,128)} %get-tuple-element.29, f32[2,2,256,256]{3,2,1,0:T(8,128)S(1)} %get-tuple-element.27, f32[2,2,256,256]{3,2,1,0:T(8,128)} %collective-permute-done.11), kind=kLoop, calls=%fused_computation.1 | loop fusion | flops 1048576 | bytes 5767168 | tf_op jit(solution)/shard_map/add | solution.py:467
  88.1 4.1 %collective-permute-done.10 = f32[264,128]{1,0:T(8,128)S(1)} collective-permute-done((f32[264,128]{1,0:T(8,128)S(1)}, f32[264,128]{1,0:T(8,128)S(1)}, u32[]{:S(2)}, u32[]{:S(2)}) %collective-permute-start.10) | collective-permute-done | bytes 135200 | tf_op jit(solution)/shard_map/ppermute | solution.py:29
  92.3 5.0 %collective-permute-done.13 = f32[264,128]{1,0:T(8,128)S(1)} collective-permute-done((f32[264,128]{1,0:T(8,128)S(1)}, f32[264,128]{1,0:T(8,128)S(1)}, u32[]{:S(2)}, u32[]{:S(2)}) %collective-permute-start.13) | collective-permute-done | bytes 135200 | tf_op jit(solution)/shard_map/ppermute | solution.py:29
  97.4 2.7 %collective-permute-start.14 = (f32[512,128]{1,0:T(8,128)S(1)}, f32[512,128]{1,0:T(8,128)S(1)}, u32[]{:S(2)}, u32[]{:S(2)}) collective-permute-start(f32[512,128]{1,0:T(8,128)S(1)} %pad_maximum_fusion.1), channel_id=1, source_target_pairs={{0,1},{1,0},{2,3},{3,2},{4,5},{5,4},{6,7},{7,6},{8,9},{9,8},{10,11... | collective-permute-start | bytes 786440 | tf_op jit(solution)/shard_map/ppermute | solution.py:29
  100.1 0.6 dynamic_slice.19
  100.7 0.6 collective-permute-done.14
  101.3 0.8 pad_maximum_fusion
  (43 shorter events, 1.3 us)
Async XLA Ops:
  0.6 7.3 %collective-permute-start = (f32[2,2,256,256]{3,2,1,0:T(8,128)}, f32[2,2,256,256]{3,2,1,0:T(8,128)S(1)}, u32[]{:S(2)}, u32[]{:S(2)}) collective-permute-start(f32[2,2,256,256]{3,2,1,0:T(8,128)} %refs_1_.3), channel_id=1, source_target_pairs={{0,1},{1,0},{2,3},{3,2},{4,5},{5,4},{6,7},{7,6},{8,9},{9,8},{10,11... | collective-permute-start | bytes 3145736 | tf_op jit(solution)/shard_map/ppermute | solution.py:29
  3.3 12.5 %collective-permute-start.1 = (f32[1032,128]{1,0:T(8,128)}, f32[1032,128]{1,0:T(8,128)S(1)}, u32[]{:S(2)}, u32[]{:S(2)}) collective-permute-start(f32[1032,128]{1,0:T(8,128)} %shard_map.94.refs_3_.packed.refs_5_), channel_id=1, source_target_pairs={{0,1},{1,0},{2,3},{3,2},{4,5},{5,4},{6,7},{7,6},{8,9},{9,8},{10,11... | collective-permute-start | bytes 1585160 | tf_op jit(solution)/shard_map/ppermute | solution.py:29
  3.8 32.1 %collective-permute-start.2 = (f32[1032,128]{1,0:T(8,128)}, f32[1032,128]{1,0:T(8,128)}, u32[]{:S(2)}, u32[]{:S(2)}) collective-permute-start(f32[1032,128]{1,0:T(8,128)} %shard_map.94.refs_3_.packed.refs_5_), channel_id=1, source_target_pairs={{0,2},{1,3},{2,4},{3,5},{4,6},{5,7},{6,8},{7,9},{8,10},{9,11},{10,... | collective-permute-start | bytes 1585160 | tf_op jit(solution)/shard_map/ppermute | solution.py:24
  7.9 7.6 %copy-start.11 = (f32[128,128]{1,0:T(8,128)S(1)}, f32[128,128]{1,0:T(8,128)}, u32[]{:S(2)}) copy-start(f32[128,128]{1,0:T(8,128)} %param.9) | copy-start | bytes 196612
  7.9 8.7 %copy-start = (f32[1032,128]{1,0:T(8,128)S(1)}, f32[1032,128]{1,0:T(8,128)}, u32[]{:S(2)}) copy-start(f32[1032,128]{1,0:T(8,128)} %shard_map.94.refs_3_.packed.refs_5_) | copy-start | bytes 1585156
  7.9 8.7 %copy-start.1 = (f32[2,2,256,256]{3,2,1,0:T(8,128)S(1)}, f32[2,2,256,256]{3,2,1,0:T(8,128)}, u32[]{:S(2)}) copy-start(f32[2,2,256,256]{3,2,1,0:T(8,128)} %refs_1_.3) | copy-start | bytes 3145732
  7.9 8.7 %copy-start.2 = (s32[3]{0:T(128)S(1)}, s32[3]{0:T(128)}, u32[]{:S(2)}) copy-start(s32[3]{0:T(128)} %pad_add_fusion.refs_0_.place) | copy-start | bytes 40
  7.9 8.7 %copy-start.9 = (f32[2,128,128]{2,1,0:T(8,128)S(1)}, f32[2,128,128]{2,1,0:T(8,128)}, u32[]{:S(2)}) copy-start(f32[2,128,128]{2,1,0:T(8,128)} %constant.76.clone.refs_7_.refs_12_) | copy-start | bytes 393220
  7.9 1.0 copy-start.10
  12.1 25.5 %collective-permute-start.3 = (f32[1544,128]{1,0:T(8,128)}, f32[1544,128]{1,0:T(8,128)S(1)}, u32[]{:S(2)}, u32[]{:S(2)}) collective-permute-start(f32[1544,128]{1,0:T(8,128)} %shard_map.96), channel_id=1, source_target_pairs={{2,0},{3,1},{4,2},{5,3},{6,4},{7,5},{8,6},{9,7},{10,8},{11,9},{12,... | collective-permute-start | bytes 2371592 | tf_op jit(solution)/shard_map/ppermute | solution.py:24
  15.7 0.8 copy-start.5
  16.6 1.0 %copy-start.6 = (f32[1032,128]{1,0:T(8,128)S(1)}, f32[1032,128]{1,0:T(8,128)}, u32[]{:S(2)}) copy-start(f32[1032,128]{1,0:T(8,128)} %copy-done.5) | copy-start | bytes 1585156
  17.6 1.0 %copy-start.7 = (f32[4,2,128,128]{3,2,1,0:T(8,128)S(1)}, f32[4,2,128,128]{3,2,1,0:T(8,128)}, u32[]{:S(2)}) copy-start(f32[4,2,128,128]{3,2,1,0:T(8,128)} %refs_10_.1) | copy-start | bytes 1572868
  18.7 22.0 %copy-start.8 = (f32[4,2,128,128]{3,2,1,0:T(8,128)S(1)}, f32[4,2,128,128]{3,2,1,0:T(8,128)}, u32[]{:S(2)}) copy-start(f32[4,2,128,128]{3,2,1,0:T(8,128)} %refs_10_.1) | copy-start | bytes 1572868
  25.7 1.0 copy-start.3
  37.6 19.1 %copy-start.4 = (f32[2,2,256,256]{3,2,1,0:T(8,128)S(1)}, f32[2,2,256,256]{3,2,1,0:T(8,128)}, u32[]{:S(2)}) copy-start(f32[2,2,256,256]{3,2,1,0:T(8,128)} %copy-done.3) | copy-start | bytes 3145732
  37.6 3.1 %collective-permute-start.5 = (f32[1544,128]{1,0:T(8,128)S(1)}, f32[1544,128]{1,0:T(8,128)S(1)}, u32[]{:S(2)}, u32[]{:S(2)}) collective-permute-start(f32[1544,128]{1,0:T(8,128)S(1)} %collective-permute-done.3.refs_7_), channel_id=1, source_target_pairs={{0,1},{1,0},{2,3},{3,2},{4,5},{5,4},{6,7},{7,6},{8,9},{9,8},{10,11... | collective-permute-start | bytes 2371592 | tf_op jit(solution)/shard_map/ppermute | solution.py:29
  37.6 3.0 %collective-permute-start.4 = (f32[1032,128]{1,0:T(8,128)}, f32[1032,128]{1,0:T(8,128)S(1)}, u32[]{:S(2)}, u32[]{:S(2)}) collective-permute-start(f32[1032,128]{1,0:T(8,128)} %collective-permute-done.2.refs_3_), channel_id=1, source_target_pairs={{0,1},{1,0},{2,3},{3,2},{4,5},{5,4},{6,7},{7,6},{8,9},{9,8},{10,11... | collective-permute-start | bytes 1585160 | tf_op jit(solution)/shard_map/ppermute | solution.py:29
  56.1 6.8 %collective-permute-start.8 = (f32[2,2,384,256]{3,2,1,0:T(8,128)}, f32[2,2,384,256]{3,2,1,0:T(8,128)}, u32[]{:S(2)}, u32[]{:S(2)}) collective-permute-start(f32[2,2,384,256]{3,2,1,0:T(8,128)} %get-tuple-element.25), channel_id=1, source_target_pairs={{0,1},{1,0},{2,3},{3,2},{4,5},{5,4},{6,7},{7,6},{8,9},{9,8},{10,11... | collective-permute-start | bytes 4718600 | tf_op jit(solution)/shard_map/ppermute | solution.py:29
  56.4 3.9 %collective-permute-start.6 = (f32[528,128]{1,0:T(8,128)S(1)}, f32[528,128]{1,0:T(8,128)S(1)}, u32[]{:S(2)}, u32[]{:S(2)}) collective-permute-start(f32[528,128]{1,0:T(8,128)S(1)} %constant_dynamic-slice_fusion.1), channel_id=1, source_target_pairs={{0,1},{1,0},{2,3},{3,2},{4,5},{5,4},{6,7},{7,6},{8,9},{9,8},{10,11... | collective-permute-start | bytes 811016 | tf_op jit(solution)/shard_map/ppermute | solution.py:29
  56.7 28.1 %collective-permute-start.11 = (f32[2,2,256,256]{3,2,1,0:T(8,128)S(1)}, f32[2,2,256,256]{3,2,1,0:T(8,128)}, u32[]{:S(2)}, u32[]{:S(2)}) collective-permute-start(f32[2,2,256,256]{3,2,1,0:T(8,128)S(1)} %copy-done.4), channel_id=1, source_target_pairs={{0,1},{1,0},{2,3},{3,2},{4,5},{5,4},{6,7},{7,6},{8,9},{9,8},{10,11... | collective-permute-start | bytes 3145736 | tf_op jit(solution)/shard_map/ppermute | solution.py:29
  60.4 6.6 %collective-permute-start.7 = (f32[264,128]{1,0:T(8,128)S(1)}, f32[264,128]{1,0:T(8,128)S(1)}, u32[]{:S(2)}, u32[]{:S(2)}) collective-permute-start(f32[264,128]{1,0:T(8,128)S(1)} %constant_dynamic-slice_fusion), channel_id=1, source_target_pairs={{0,2},{1,3},{2,0},{3,1},{4,6},{5,7},{6,4},{7,5},{8,10},{9,11},{10,... | collective-permute-start | bytes 405512 | tf_op jit(solution)/shard_map/ppermute | solution.py:29
  67.0 17.9 %collective-permute-start.12 = (f32[2,2,128,256]{3,2,1,0:T(8,128)S(1)}, f32[2,2,128,256]{3,2,1,0:T(8,128)}, u32[]{:S(2)}, u32[]{:S(2)}) collective-permute-start(f32[2,2,128,256]{3,2,1,0:T(8,128)S(1)} %slice_add_fusion.1), channel_id=1, source_target_pairs={{1,2},{3,4},{5,6},{7,8},{9,10},{11,12},{13,14},{17,18},{19,20},{21... | collective-permute-start | bytes 1572872 | tf_op jit(solution)/shard_map/ppermute | solution.py:466
  68.3 16.4 %collective-permute-start.9 = (f32[264,128]{1,0:T(8,128)S(1)}, f32[264,128]{1,0:T(8,128)S(1)}, u32[]{:S(2)}, u32[]{:S(2)}) collective-permute-start(f32[264,128]{1,0:T(8,128)S(1)} %dynamic-slice_add_fusion.1), channel_id=1, source_target_pairs={{0,4},{1,5},{2,6},{3,7},{4,0},{5,1},{6,2},{7,3},{8,12},{9,13},{10,... | collective-permute-start | bytes 405512 | tf_op jit(solution)/shard_map/ppermute | solution.py:29
  84.7 7.5 %collective-permute-start.10 = (f32[264,128]{1,0:T(8,128)S(1)}, f32[264,128]{1,0:T(8,128)S(1)}, u32[]{:S(2)}, u32[]{:S(2)}) collective-permute-start(f32[264,128]{1,0:T(8,128)S(1)} %add.66), channel_id=1, source_target_pairs={{0,8},{1,9},{2,10},{3,11},{4,12},{5,13},{6,14},{7,15},{8,0},{9,1},... | collective-permute-start | bytes 405512 | tf_op jit(solution)/shard_map/ppermute | solution.py:29
  92.3 5.1 %collective-permute-start.13 = (f32[264,128]{1,0:T(8,128)S(1)}, f32[264,128]{1,0:T(8,128)S(1)}, u32[]{:S(2)}, u32[]{:S(2)}) collective-permute-start(f32[264,128]{1,0:T(8,128)S(1)} %add.71), channel_id=1, source_target_pairs={{0,2},{1,3},{2,0},{3,1},{4,6},{5,7},{6,4},{7,5},{8,10},{9,11},{10,... | collective-permute-start | bytes 405512 | tf_op jit(solution)/shard_map/ppermute | solution.py:29
  97.4 3.9 %collective-permute-start.14 = (f32[512,128]{1,0:T(8,128)S(1)}, f32[512,128]{1,0:T(8,128)S(1)}, u32[]{:S(2)}, u32[]{:S(2)}) collective-permute-start(f32[512,128]{1,0:T(8,128)S(1)} %pad_maximum_fusion.1), channel_id=1, source_target_pairs={{0,1},{1,0},{2,3},{3,2},{4,5},{5,4},{6,7},{7,6},{8,9},{9,8},{10,11... | collective-permute-start | bytes 786440 | tf_op jit(solution)/shard_map/ppermute | solution.py:29
